TPU v7x, 512 devices: a whole 4x8x8 slice. The times are simulated.
512 devices in a mesh: dom: 128 (over z, y, core), grp: 4 (over x).
Axes of the slice: x: 4, y: 8, z: 8, core: 2. Of those that a mesh axis runs over, the one named last changes fastest.
Arguments:
- source_emb: float32 [400, 65536], P(None, ('dom', 'grp')), may hold values from -2.5 to 2.5
- source_state: float32 [65536], P(('dom', 'grp')), may hold values from 0.005 to 0.1
- dest_emb: float32 [400, 65536], P(None, ('dom', 'grp')), may hold values from -2.5 to 2.5
- dest_state: float32 [65536], P(('dom', 'grp')), may hold values from 0.005 to 0.1
- relations: float32 [400, 768], replicated, may hold values from -4 to 4
- relation_state: float32 [768], replicated, may hold values from 1 to 30
- partner: int32 [128, 4], P('dom', 'grp'), may hold values from 0 to 127, as said below
- edge_count: int32 [128, 4], P('dom', 'grp'), may hold values from 1 to 1024, as said below
- source_rows: int32 [128, 4, 1024], P('dom', 'grp'), may hold values from 0 to 127
- target_rows: int32 [128, 4, 1024], P('dom', 'grp'), may hold values from 0 to 127
- relation_index: int32 [128, 4, 1024], P('dom', 'grp'), may hold values from 0 to 767
- negative_rows: int32 [128, 4, 2048], P('dom', 'grp'), may hold values from 0 to 127
Outputs:
- source_out: float32 [400, 65536], P(None, ('dom', 'grp'))
- source_state_out: float32 [65536], P(('dom', 'grp'))
- dest_out: float32 [400, 65536], P(None, ('dom', 'grp'))
- dest_state_out: float32 [65536], P(('dom', 'grp'))
- relations_out: float32 [400, 768], replicated
- relation_state_out: float32 [768], replicated
Inputs may be any that keep to these rules, and one draw needn't show every extreme that they name: For each grp index g, partner[:, g] is a permutation of 0 .. 127. `edge_count`: some device has all 1024 edges live.
All inputs are finite; a program needn't handle non-finite values.
Results may differ from a plain program's by a relative error of at most 0.0013.
The roundings to bfloat16 on the way count: a program that leaves them out, or rounds other values in their place, can miss the bound.
Values sent between devices are 32-bit elements; how exact they have to be, the bound alone decides.
No kernel may reach another device: no remote copies, remote signals or barrier semaphores. Data moves between devices by JAX's collectives and lax.ppermute only.
A program may use at most 64 MiB of HBM per device.

v0:
```python
import jax
import jax.numpy as jnp
from jax import lax
from jax.sharding import PartitionSpec as P

SPAN = 512
SPANS = 2
NEG = 1024
EDGES = 1024
learn_rate = 0.3
epsilon = 1e-08


def passed_along(value, axis, steps):
    count = lax.axis_size(axis)
    pairs = [(source, (source + steps) % count) for source in range(count)]
    return lax.ppermute(value, axis, pairs)


def adagrad(param, state, grad):
    new_state = state + jnp.mean(grad * grad, axis=0)
    return (param - learn_rate * grad / (jnp.sqrt(new_state) + epsilon), new_state)


def contract_last(left, right):
    return lax.dot_general(
        left, right, (((1,), (1,)), ((), ())), preferred_element_type=jnp.float32
    )


def selector(count, rows):
    return (jnp.arange(count, dtype=jnp.int32)[:, None] == rows[None, :]).astype(jnp.bfloat16)


def train_block(
    source, source_acc, target, target_acc, relation_bf, rows_s, rows_t, rows_r, rows_n, live
):
    width = source.shape[0]
    half = width // 2
    block = source.shape[1]
    pick_source = selector(block, rows_s)
    pick_target = selector(block, rows_t)
    pick_noise = selector(block, rows_n)
    pick_relation = selector(relation_bf.shape[1], rows_r)
    source_bf = source.astype(jnp.bfloat16)
    target_bf = target.astype(jnp.bfloat16)
    subject = jnp.dot(source_bf, pick_source, preferred_element_type=jnp.float32)
    operator = jnp.dot(relation_bf, pick_relation, preferred_element_type=jnp.float32)
    objects = jnp.dot(target_bf, pick_target, preferred_element_type=jnp.float32)
    noise = jnp.dot(target_bf, pick_noise, preferred_element_type=jnp.float32).astype(jnp.bfloat16)
    subject_re, subject_im = (subject[:half], subject[half:])
    operator_re, operator_im = (operator[:half], operator[half:])
    query = jnp.concatenate(
        [
            subject_re * operator_re - subject_im * operator_im,
            subject_re * operator_im + subject_im * operator_re,
        ],
        0,
    )
    positive = jnp.sum(query * objects, axis=0)
    query_bf = query.astype(jnp.bfloat16)
    negative = lax.dot_general(
        query_bf, noise, (((0,), (0,)), ((), ())), preferred_element_type=jnp.float32
    )
    grad_pos = -jax.nn.sigmoid(-positive) * live
    grad_neg = (jax.nn.sigmoid(negative) * (live[:, None] / NEG)).astype(jnp.bfloat16)
    grad_query = grad_pos[None, :] * objects + contract_last(noise, grad_neg)
    grad_objects = grad_pos[None, :] * query
    grad_noise = jnp.dot(query_bf, grad_neg, preferred_element_type=jnp.float32)
    query_gre, query_gim = (grad_query[:half], grad_query[half:])
    grad_subject = jnp.concatenate(
        [
            query_gre * operator_re + query_gim * operator_im,
            query_gim * operator_re - query_gre * operator_im,
        ],
        0,
    )
    grad_operator = jnp.concatenate(
        [
            query_gre * subject_re + query_gim * subject_im,
            query_gim * subject_re - query_gre * subject_im,
        ],
        0,
    )
    grad_source = contract_last(grad_subject.astype(jnp.bfloat16), pick_source)
    grad_target = contract_last(grad_objects.astype(jnp.bfloat16), pick_target)
    grad_target = grad_target + contract_last(grad_noise.astype(jnp.bfloat16), pick_noise)
    grad_local = contract_last(grad_operator.astype(jnp.bfloat16), pick_relation)
    new_source, new_source_acc = adagrad(source, source_acc, grad_source)
    new_target, new_target_acc = adagrad(target, target_acc, grad_target)
    return (new_source, new_source_acc, new_target, new_target_acc, grad_local)


def relation_step(relations, relation_state, grad_local):
    total = lax.psum(grad_local, ("dom", "grp"))
    return adagrad(relations, relation_state, total)


def local(
    source_emb,
    source_state,
    dest_emb,
    dest_state,
    relations,
    relation_state,
    partner,
    edge_count,
    source_rows,
    target_rows,
    relation_index,
    negative_rows,
):
    width = source_emb.shape[0]
    block = source_emb.shape[1]
    members = lax.axis_size("dom")
    piece = block // members
    cargo = jnp.concatenate([dest_emb, dest_state[None, :]], 0)
    cargo = passed_along(cargo, "grp", 1)
    partners = lax.all_gather(partner[0], "dom", axis=0, tiled=True)
    spread = lax.all_to_all(
        cargo.reshape(width + 1, members, piece), "dom", split_axis=1, concat_axis=1, tiled=True
    )
    spread = jnp.take(spread, partners, axis=1)
    arrived = lax.all_to_all(spread, "dom", split_axis=1, concat_axis=1, tiled=True).reshape(
        width + 1, block
    )
    target = arrived[:width]
    target_acc = arrived[width]
    source = source_emb
    source_acc = source_state
    live_all = (jnp.arange(EDGES, dtype=jnp.int32) < edge_count[0, 0]).astype(jnp.float32)
    for step in range(SPANS):
        first = step * SPAN
        first_neg = step * NEG
        relation_bf = relations.astype(jnp.bfloat16)
        source, source_acc, target, target_acc, grad_local = train_block(
            source,
            source_acc,
            target,
            target_acc,
            relation_bf,
            source_rows[0, 0, first : first + SPAN],
            target_rows[0, 0, first : first + SPAN],
            relation_index[0, 0, first : first + SPAN],
            negative_rows[0, 0, first_neg : first_neg + NEG],
            live_all[first : first + SPAN],
        )
        relations, relation_state = relation_step(relations, relation_state, grad_local)
    cargo = jnp.concatenate([target, target_acc[None, :]], 0).reshape(width + 1, members, piece)
    collected = lax.all_to_all(cargo, "dom", split_axis=1, concat_axis=1, tiled=True)
    inverse = (
        jnp.zeros((members,), jnp.int32).at[partners].set(jnp.arange(members, dtype=jnp.int32))
    )
    collected = jnp.take(collected, inverse, axis=1)
    returned = lax.all_to_all(collected, "dom", split_axis=1, concat_axis=1, tiled=True).reshape(
        width + 1, block
    )
    settled = passed_along(returned, "grp", -1)
    return (source, source_acc, settled[:width], settled[width], relations, relation_state)


def solution(mesh):
    in_specs = (
        P(None, ("dom", "grp")),
        P(("dom", "grp")),
        P(None, ("dom", "grp")),
        P(("dom", "grp")),
        P(),
        P(),
        P("dom", "grp"),
        P("dom", "grp"),
        P("dom", "grp", None),
        P("dom", "grp", None),
        P("dom", "grp", None),
        P("dom", "grp", None),
    )
    out_specs = (
        P(None, ("dom", "grp")),
        P(("dom", "grp")),
        P(None, ("dom", "grp")),
        P(("dom", "grp")),
        P(),
        P(),
    )
    return jax.shard_map(local, mesh=mesh, in_specs=in_specs, out_specs=out_specs, check_vma=False)
```

profile of v0, /device:TPU:23, one launch (start us, length us, event | category | flops | bytes accessed | tf_op | source)
XLA Modules:
  0.0 705.2 jit_solution(11849376523727967690)
XLA Ops:
  8.2 2.1 collective-permute-start
  13.0 27.1 %all-reduce = s32[128]{0:T(128)S(1)} all-reduce(s32[128]{0:T(128)S(1)} %bitcast_dynamic-update-slice_fusion), channel_id=2, replica_groups=mesh['dom'=128,'grp'=4] {'dom'}, use_global_device_ids=true, to_apply=%add | all-reduce | flops 128 | bytes 1024 | tf_op jit(solution)/shard_map/all_gather | solution.py:119
  45.9 11.1 %all-to-all-start = ((f32[401,128,1]{0,2,1:T(1,128)}), f32[401,128,1]{0,2,1:T(1,128)S(1)}, u32[]{:S(2)}, u32[]{:S(2)}) async-start(f32[401,128,1]{0,2,1:T(1,128)} %copy.35), calls=%async_computation | async-start | bytes 524288 | tf_op jit(solution)/shard_map/all_to_all | solution.py:120
  58.2 11.9 %all-to-all-done = f32[401,128,1]{0,2,1:T(1,128)S(1)} async-done(((f32[401,128,1]{0,2,1:T(1,128)}), f32[401,128,1]{0,2,1:T(1,128)S(1)}, u32[]{:S(2)}, u32[]{:S(2)}) %all-to-all-start) | async-done | bytes 205344 | tf_op jit(solution)/shard_map/all_to_all | solution.py:120
  71.9 8.8 %all-to-all-start.1 = ((f32[401,128,1]{0,2,1:T(1,128)}), f32[401,128,1]{0,2,1:T(1,128)}, u32[]{:S(2)}, u32[]{:S(2)}) async-start(f32[401,128,1]{0,2,1:T(1,128)} %copy.38), calls=%async_computation.1 | async-start | bytes 524288 | tf_op jit(solution)/shard_map/all_to_all | solution.py:124
  81.9 11.6 %all-to-all-done.1 = f32[401,128,1]{0,2,1:T(1,128)} async-done(((f32[401,128,1]{0,2,1:T(1,128)}), f32[401,128,1]{0,2,1:T(1,128)}, u32[]{:S(2)}, u32[]{:S(2)}) %all-to-all-start.1) | async-done | bytes 205344 | tf_op jit(solution)/shard_map/all_to_all | solution.py:124
  97.8 2.0 multiply_convert_fusion.1
  99.8 2.9 multiply_reduce_fusion.6
  102.7 2.3 convolution_add_fusion.1
  105.4 1.6 fusion.2
  107.3 2.7 slice_reduce_fusion
  111.7 264.1 %all-reduce.4.cloned.1.call-done = f32[400,768]{1,0:T(8,128)} async-done(((f32[400,768]{1,0:T(8,128)}), f32[400,768]{1,0:T(8,128)}) %all-reduce.4.cloned.1.call-update) | async-done | bytes 1228816 | tf_op jit(solution)/shard_map/psum | solution.py:95
  375.8 1.5 multiply_reduce_fusion.1
  381.2 2.0 multiply_convert_fusion
  383.2 3.0 multiply_reduce_fusion.4
  386.2 2.4 convolution_add_fusion
  390.8 9.6 %all-to-all-start.2 = ((f32[401,128,1]{0,2,1:T(1,128)}), f32[401,128,1]{0,2,1:T(1,128)S(1)}, u32[]{:S(2)}, u32[]{:S(2)}) async-start(f32[401,128,1]{0,2,1:T(1,128)} %copy.40), calls=%async_computation.2 | async-start | bytes 524288 | tf_op jit(solution)/shard_map/all_to_all | solution.py:150
  400.5 2.6 fusion
  403.9 9.6 %all-to-all-done.2 = f32[401,128,1]{0,2,1:T(1,128)S(1)} async-done(((f32[401,128,1]{0,2,1:T(1,128)}), f32[401,128,1]{0,2,1:T(1,128)S(1)}, u32[]{:S(2)}, u32[]{:S(2)}) %all-to-all-start.2) | async-done | bytes 205344 | tf_op jit(solution)/shard_map/all_to_all | solution.py:150
  415.3 7.7 %all-to-all-start.3 = ((f32[401,128,1]{0,2,1:T(1,128)}), f32[401,128,1]{0,2,1:T(1,128)S(1)}, u32[]{:S(2)}, u32[]{:S(2)}) async-start(f32[401,128,1]{0,2,1:T(1,128)} %copy.43), calls=%async_computation.3 | async-start | bytes 524288 | tf_op jit(solution)/shard_map/all_to_all | solution.py:155
  423.8 261.1 %all-reduce.6.cloned.1.call-done = f32[400,768]{1,0:T(8,128)} async-done(((f32[400,768]{1,0:T(8,128)}), f32[400,768]{1,0:T(8,128)}) %all-reduce.6.cloned.1.call-update) | async-done | bytes 1228816 | tf_op jit(solution)/shard_map/psum | solution.py:95
  687.0 2.3 collective-permute-start.1
  689.3 2.6 divide_subtract_fusion
  691.9 5.2 collective-permute-done.1
  (107 shorter events, 31.7 us)
Async XLA Ops:
  7.2 50.5 %copy-start = (f32[400,768]{1,0:T(8,128)S(1)}, f32[400,768]{1,0:T(8,128)}, u32[]{:S(2)}) copy-start(f32[400,768]{1,0:T(8,128)} %param.18) | copy-start | bytes 3686404
  8.2 36.8 %collective-permute-start = (f32[401,128]{1,0:T(8,128)S(1)}, f32[401,128]{1,0:T(8,128)S(1)}, u32[]{:S(2)}, u32[]{:S(2)}) collective-permute-start(f32[401,128]{1,0:T(8,128)S(1)} %pad_maximum_fusion.2), channel_id=1, source_target_pairs={{0,1},{1,2},{2,3},{3,0},{4,5},{5,6},{6,7},{7,4},{8,9},{9,10},{10,1... | collective-permute-start | bytes 615944 | tf_op jit(solution)/shard_map/ppermute | solution.py:17
  45.9 24.2 %all-to-all-start = ((f32[401,128,1]{0,2,1:T(1,128)}), f32[401,128,1]{0,2,1:T(1,128)S(1)}, u32[]{:S(2)}, u32[]{:S(2)}) async-start(f32[401,128,1]{0,2,1:T(1,128)} %copy.35), calls=%async_computation | async-start | bytes 524288 | tf_op jit(solution)/shard_map/all_to_all | solution.py:120
  71.9 21.6 %all-to-all-start.1 = ((f32[401,128,1]{0,2,1:T(1,128)}), f32[401,128,1]{0,2,1:T(1,128)}, u32[]{:S(2)}, u32[]{:S(2)}) async-start(f32[401,128,1]{0,2,1:T(1,128)} %copy.38), calls=%async_computation.1 | async-start | bytes 524288 | tf_op jit(solution)/shard_map/all_to_all | solution.py:124
  80.7 295.1 %all-reduce.4.cloned.1.call-start = ((), (), s32[]{:S(2)}) async-start(), calls=%async_computation.4 | async-start | bytes 2457600 | tf_op jit(solution)/shard_map/psum | solution.py:95
  95.0 2.8 copy-start.5
  106.9 3.1 copy-start.16
  107.0 3.1 copy-start.19
  107.0 4.4 copy-start.6
  107.3 4.1 copy-start.11
  111.4 265.9 %copy-start.18 = (f32[768]{0:T(1024)S(1)}, f32[768]{0:T(1024)}, u32[]{:S(2)}) copy-start(f32[768]{0:T(1024)} %param.19) | copy-start | bytes 9220
  378.3 2.9 copy-start.9
  378.3 2.9 copy-start.10
  379.0 2.2 copy-start.4
  386.2 2.4 copy-start.3
  389.9 10.5 %copy-start.15 = (bf16[200,512]{1,0:T(8,128)(2,1)S(1)}, bf16[200,512]{1,0:T(8,128)(2,1)}, u32[]{:S(2)}) copy-start(bf16[200,512]{1,0:T(8,128)(2,1)} %get-tuple-element.29) | copy-start | bytes 614404
  390.8 22.6 %all-to-all-start.2 = ((f32[401,128,1]{0,2,1:T(1,128)}), f32[401,128,1]{0,2,1:T(1,128)S(1)}, u32[]{:S(2)}, u32[]{:S(2)}) async-start(f32[401,128,1]{0,2,1:T(1,128)} %copy.40), calls=%async_computation.2 | async-start | bytes 524288 | tf_op jit(solution)/shard_map/all_to_all | solution.py:150
  400.4 284.5 %all-reduce.6.cloned.1.call-start = ((), (), s32[]{:S(2)}) async-start(), calls=%async_computation.5 | async-start | bytes 2457600 | tf_op jit(solution)/shard_map/psum | solution.py:95
  400.4 2.6 copy-start.13
  400.4 2.6 copy-start.14
  414.2 8.8 %copy-start.7 = (f32[400,128]{1,0:T(8,128)S(1)}, f32[400,128]{1,0:T(8,128)}, u32[]{:S(2)}) copy-start(f32[400,128]{1,0:T(8,128)} %param.14) | copy-start | bytes 614404
  414.2 8.8 %copy-start.12 = (f32[400,128]{1,0:T(8,128)S(1)}, f32[400,128]{1,0:T(8,128)}, u32[]{:S(2)}) copy-start(f32[400,128]{1,0:T(8,128)} %copy-done.11) | copy-start | bytes 614404
  415.3 271.6 %all-to-all-start.3 = ((f32[401,128,1]{0,2,1:T(1,128)}), f32[401,128,1]{0,2,1:T(1,128)S(1)}, u32[]{:S(2)}, u32[]{:S(2)}) async-start(f32[401,128,1]{0,2,1:T(1,128)} %copy.43), calls=%async_computation.3 | async-start | bytes 524288 | tf_op jit(solution)/shard_map/all_to_all | solution.py:155
  687.0 10.1 %collective-permute-start.1 = (f32[401,128]{1,0:T(8,128)S(1)}, f32[401,128]{1,0:T(8,128)S(1)}, u32[]{:S(2)}, u32[]{:S(2)}) collective-permute-start(f32[401,128]{1,0:T(8,128)S(1)} %bitcast.84), channel_id=1, source_target_pairs={{0,3},{1,0},{2,1},{3,2},{4,7},{5,4},{6,5},{7,6},{8,11},{9,8},{10,9... | collective-permute-start | bytes 615944 | tf_op jit(solution)/shard_map/ppermute | solution.py:17
  (4 other events, 4.9 us)
Sparse Core Ops, SparseCore 0:
  107.1 268.6 all-reduce.3
  407.7 277.1 all-reduce.5
where the time goes:
time: 706 us; the launch traced here: 705 us
  waiting for transfers between devices  564 us (80%)
  starting transfers between devices  41.8 us (6%)
  matrix products  27.9 us (4%)
  blocking collectives  27.1 us (4%)
  local copies, waits for them, and re-layouts  17.5 us (2%)
  between operations  15.8 us (2%)
  other arithmetic  11.5 us (2%)
    psum x2, waiting for transfers between devices, relation_step(): total = lax.psum(grad_local, ('dom', 'grp'))  525 us
    all_gather x1, blocking collectives, local(): partners = lax.all_gather(partner[0], 'dom', axis=0, tiled=True)  27.1 us
    dot_general x10, matrix products, contract_last(): lax.dot_general(left, right, (((1,), (1,)), ((), ())), preferred_element_...  17.3 us
  transfers between devices with their start and end apart: 8, of which 6 were waited for; matrix products, arithmetic and copies ran while one was open for 3% of the time, Pallas kernels for 0%

commit v1 on v0

--- a/solution.py
+++ b/solution.py
@@ -117,9 +117,11 @@
     cargo = jnp.concatenate([dest_emb, dest_state[None, :]], 0)
     cargo = passed_along(cargo, "grp", 1)
     partners = lax.all_gather(partner[0], "dom", axis=0, tiled=True)
-    spread = lax.all_to_all(
-        cargo.reshape(width + 1, members, piece), "dom", split_axis=1, concat_axis=1, tiled=True
-    )
+    x = cargo.reshape(width + 1, members, piece)
+    size = lax.axis_size("dom")
+    blocks = jnp.stack(jnp.split(x, size, axis=1), axis=0)
+    blocks = lax.all_to_all(blocks, "dom", split_axis=0, concat_axis=0)
+    spread = jnp.concatenate(blocks, axis=1)
     spread = jnp.take(spread, partners, axis=1)
     arrived = lax.all_to_all(spread, "dom", split_axis=1, concat_axis=1, tiled=True).reshape(
         width + 1, block

time: 706 us -> 806 us (1.14); the launches traced: 705 us -> 796 us
  local copies, waits for them, and re-layouts: 17.5 us -> 108 us
    unnamed x44 -> x173, local copies, waits for them, and re-layouts: 4.52 us -> 78 us
    split x0 -> x7, local copies, waits for them, and re-layouts: none -> 16.8 us  [local(): blocks = jnp.stack(jnp.split(x, size, axis=1), axis=0)]
where the time goes in v1:
time: 806 us; the launch traced here: 796 us
  waiting for transfers between devices  562 us (70%)
  local copies, waits for them, and re-layouts  108 us (13%)
  starting transfers between devices  41.8 us (5%)
  matrix products  28.6 us (4%)
  blocking collectives  27.1 us (3%)
  between operations  16.1 us (2%)
  other arithmetic  13 us (2%)
    psum x2, waiting for transfers between devices, relation_step(): total = lax.psum(grad_local, ('dom', 'grp'))  524 us
    unnamed x173, local copies, waits for them, and re-layouts  78 us
    all_gather x1, blocking collectives, local(): partners = lax.all_gather(partner[0], 'dom', axis=0, tiled=True)  27.1 us
    dot_general x10, matrix products, contract_last(): lax.dot_general(left, right, (((1,), (1,)), ((), ())), preferred_element_...  17.9 us
    split x7, local copies, waits for them, and re-layouts, local(): blocks = jnp.stack(jnp.split(x, size, axis=1), axis=0)  16.8 us
  transfers between devices with their start and end apart: 8, of which 6 were waited for; matrix products, arithmetic and copies ran while one was open for 3% of the time, Pallas kernels for 0%

profile of v1, /device:TPU:23, one launch (start us, length us, event | category | flops | bytes accessed | tf_op | source)
XLA Modules:
  0.0 796.2 jit_solution(15902560031424962784)
XLA Ops:
  12.8 27.1 %all-reduce = s32[128]{0:T(128)S(1)} all-reduce(s32[128]{0:T(128)S(1)} %bitcast_dynamic-update-slice_fusion), channel_id=2, replica_groups=mesh['dom'=128,'grp'=4] {'dom'}, use_global_device_ids=true, to_apply=%add | all-reduce | flops 128 | bytes 1024 | tf_op jit(solution)/shard_map/all_gather | solution.py:119
  46.7 2.4 slice_reduce_fusion.19
  49.2 2.4 slice_reduce_fusion.76
  51.6 2.4 slice_reduce_fusion.38
  54.0 2.4 slice_reduce_fusion.57
  56.5 2.9 slice_reduce_fusion
  59.4 2.4 slice_reduce_fusion.95
  135.9 11.1 %all-to-all-start = ((f32[128,401,1,1]{1,3,2,0:T(1,128)}), f32[128,401,1,1]{1,3,2,0:T(1,128)S(1)}, u32[]{:S(2)}, u32[]{:S(2)}) async-start(f32[128,401,1,1]{1,3,2,0:T(1,128)} %constant_dynamic-update-slice_fusion), calls=%async_computation | async-start | bytes 524288 | tf_op jit(solution)/shard_map/all_to_all | solution.py:123
  148.2 11.9 %all-to-all-done = f32[128,401,1,1]{1,3,2,0:T(1,128)S(1)} async-done(((f32[128,401,1,1]{1,3,2,0:T(1,128)}), f32[128,401,1,1]{1,3,2,0:T(1,128)S(1)}, u32[]{:S(2)}, u32[]{:S(2)}) %all-to-all-start) | async-done | bytes 205344 | tf_op jit(solution)/shard_map/all_to_all | solution.py:123
  161.9 8.8 %all-to-all-start.1 = ((f32[401,128,1]{0,2,1:T(1,128)}), f32[401,128,1]{0,2,1:T(1,128)}, u32[]{:S(2)}, u32[]{:S(2)}) async-start(f32[401,128,1]{0,2,1:T(1,128)} %copy.159), calls=%async_computation.1 | async-start | bytes 524288 | tf_op jit(solution)/shard_map/all_to_all | solution.py:126
  171.8 11.7 %all-to-all-done.1 = f32[401,128,1]{0,2,1:T(1,128)} async-done(((f32[401,128,1]{0,2,1:T(1,128)}), f32[401,128,1]{0,2,1:T(1,128)}, u32[]{:S(2)}, u32[]{:S(2)}) %all-to-all-start.1) | async-done | bytes 205344 | tf_op jit(solution)/shard_map/all_to_all | solution.py:126
  189.8 2.9 multiply_reduce_fusion.6
  192.6 2.3 convolution_add_fusion.1
  197.9 2.7 slice_reduce_fusion.128
  202.4 264.1 %all-reduce.4.cloned.1.call-done = f32[400,768]{1,0:T(8,128)} async-done(((f32[400,768]{1,0:T(8,128)}), f32[400,768]{1,0:T(8,128)}) %all-reduce.4.cloned.1.call-update) | async-done | bytes 1228816 | tf_op jit(solution)/shard_map/psum | solution.py:95
  473.8 3.0 multiply_reduce_fusion.4
  476.8 2.4 convolution_add_fusion
  481.5 9.5 %all-to-all-start.2 = ((f32[401,128,1]{0,2,1:T(1,128)}), f32[401,128,1]{0,2,1:T(1,128)S(1)}, u32[]{:S(2)}, u32[]{:S(2)}) async-start(f32[401,128,1]{0,2,1:T(1,128)} %copy.161), calls=%async_computation.2 | async-start | bytes 524288 | tf_op jit(solution)/shard_map/all_to_all | solution.py:152
  491.1 2.6 fusion
  495.2 8.9 %all-to-all-done.2 = f32[401,128,1]{0,2,1:T(1,128)S(1)} async-done(((f32[401,128,1]{0,2,1:T(1,128)}), f32[401,128,1]{0,2,1:T(1,128)S(1)}, u32[]{:S(2)}, u32[]{:S(2)}) %all-to-all-start.2) | async-done | bytes 205344 | tf_op jit(solution)/shard_map/all_to_all | solution.py:152
  506.0 7.7 all-to-all-start.3
  515.4 260.2 %all-reduce.6.cloned.1.call-done = f32[400,768]{1,0:T(8,128)} async-done(((f32[400,768]{1,0:T(8,128)}), f32[400,768]{1,0:T(8,128)}) %all-reduce.6.cloned.1.call-update) | async-done | bytes 1228816 | tf_op jit(solution)/shard_map/psum | solution.py:95
  780.1 2.6 divide_subtract_fusion
  782.7 5.2 collective-permute-done.1
  (243 shorter events, 120.4 us)
Async XLA Ops:
  8.1 36.8 %collective-permute-start = (f32[401,128]{1,0:T(8,128)S(1)}, f32[401,128]{1,0:T(8,128)S(1)}, u32[]{:S(2)}, u32[]{:S(2)}) collective-permute-start(f32[401,128]{1,0:T(8,128)S(1)} %pad_maximum_fusion.2), channel_id=1, source_target_pairs={{0,1},{1,2},{2,3},{3,0},{4,5},{5,6},{6,7},{7,4},{8,9},{9,10},{10,1... | collective-permute-start | bytes 615944 | tf_op jit(solution)/shard_map/ppermute | solution.py:17
  61.8 85.9 %copy-start = (f32[400,768]{1,0:T(8,128)S(1)}, f32[400,768]{1,0:T(8,128)}, u32[]{:S(2)}) copy-start(f32[400,768]{1,0:T(8,128)} %param.18) | copy-start | bytes 3686404
  135.9 24.2 %all-to-all-start = ((f32[128,401,1,1]{1,3,2,0:T(1,128)}), f32[128,401,1,1]{1,3,2,0:T(1,128)S(1)}, u32[]{:S(2)}, u32[]{:S(2)}) async-start(f32[128,401,1,1]{1,3,2,0:T(1,128)} %constant_dynamic-update-slice_fusion), calls=%async_computation | async-start | bytes 524288 | tf_op jit(solution)/shard_map/all_to_all | solution.py:123
  161.9 21.6 %all-to-all-start.1 = ((f32[401,128,1]{0,2,1:T(1,128)}), f32[401,128,1]{0,2,1:T(1,128)}, u32[]{:S(2)}, u32[]{:S(2)}) async-start(f32[401,128,1]{0,2,1:T(1,128)} %copy.159), calls=%async_computation.1 | async-start | bytes 524288 | tf_op jit(solution)/shard_map/all_to_all | solution.py:126
  170.7 295.8 %all-reduce.4.cloned.1.call-start = ((), (), s32[]{:S(2)}) async-start(), calls=%async_computation.4 | async-start | bytes 2457600 | tf_op jit(solution)/shard_map/psum | solution.py:95
  185.0 2.8 copy-start.5
  197.6 3.1 copy-start.17
  197.6 3.2 copy-start.20
  197.6 4.5 copy-start.6
  197.9 4.2 copy-start.11
  202.1 265.9 %copy-start.19 = (f32[768]{0:T(1024)S(1)}, f32[768]{0:T(1024)}, u32[]{:S(2)}) copy-start(f32[768]{0:T(1024)} %param.19) | copy-start | bytes 9220
  469.6 2.2 copy-start.9
  469.6 2.2 copy-start.10
  469.6 2.2 copy-start.4
  476.8 2.4 copy-start.3
  480.6 10.5 %copy-start.15 = (bf16[200,512]{1,0:T(8,128)(2,1)S(1)}, bf16[200,512]{1,0:T(8,128)(2,1)}, u32[]{:S(2)}) copy-start(bf16[200,512]{1,0:T(8,128)(2,1)} %get-tuple-element.157) | copy-start | bytes 614404
  481.5 22.6 %all-to-all-start.2 = ((f32[401,128,1]{0,2,1:T(1,128)}), f32[401,128,1]{0,2,1:T(1,128)S(1)}, u32[]{:S(2)}, u32[]{:S(2)}) async-start(f32[401,128,1]{0,2,1:T(1,128)} %copy.161), calls=%async_computation.2 | async-start | bytes 524288 | tf_op jit(solution)/shard_map/all_to_all | solution.py:152
  491.1 284.6 %all-reduce.6.cloned.1.call-start = ((), (), s32[]{:S(2)}) async-start(), calls=%async_computation.5 | async-start | bytes 2457600 | tf_op jit(solution)/shard_map/psum | solution.py:95
  491.1 2.6 copy-start.13
  491.1 2.6 copy-start.14
  504.9 8.8 %copy-start.7 = (f32[400,128]{1,0:T(8,128)S(1)}, f32[400,128]{1,0:T(8,128)}, u32[]{:S(2)}) copy-start(f32[400,128]{1,0:T(8,128)} %param.14) | copy-start | bytes 614404
  504.9 8.8 %copy-start.12 = (f32[400,128]{1,0:T(8,128)S(1)}, f32[400,128]{1,0:T(8,128)}, u32[]{:S(2)}) copy-start(f32[400,128]{1,0:T(8,128)} %copy-done.11) | copy-start | bytes 614404
  506.0 271.7 %all-to-all-start.3 = ((f32[401,128,1]{0,2,1:T(1,128)}), f32[401,128,1]{0,2,1:T(1,128)S(1)}, u32[]{:S(2)}, u32[]{:S(2)}) async-start(f32[401,128,1]{0,2,1:T(1,128)} %copy.164), calls=%async_computation.3 | async-start | bytes 524288 | tf_op jit(solution)/shard_map/all_to_all | solution.py:157
  777.8 10.1 %collective-permute-start.1 = (f32[401,128]{1,0:T(8,128)S(1)}, f32[401,128]{1,0:T(8,128)S(1)}, u32[]{:S(2)}, u32[]{:S(2)}) collective-permute-start(f32[401,128]{1,0:T(8,128)S(1)} %bitcast.221), channel_id=1, source_target_pairs={{0,3},{1,0},{2,1},{3,2},{4,7},{5,4},{6,5},{7,6},{8,11},{9,8},{10,9... | collective-permute-start | bytes 615944 | tf_op jit(solution)/shard_map/ppermute | solution.py:17
  (5 other events, 6.5 us)
Sparse Core Ops, SparseCore 0:
  197.7 268.7 all-reduce.3
  498.3 277.2 all-reduce.5
